TPU v7x, 512 devices: a whole 4x8x8 slice. The times are simulated.
512 devices in a mesh: row: 16 (over z_hi, y), col: 32 (over x, z_lo, core).
Axes of the slice: x: 4, y: 8, z: 8 (z_hi: 2, z_lo: 4; z = z_hi * 4 + z_lo), core: 2. Of those that a mesh axis runs over, the one named last changes fastest.
Arguments:
- inputs: bfloat16 [512, 14848], P('col', 'row'), may hold values from -6 to 6
- weight: bfloat16 [14848, 29696], P('row', 'col'), may hold values from -0.046875 to 0.046875
- cotangent: bfloat16 [512, 29696], P('row', 'col'), may hold values from -6 to 6
Outputs:
- output: bfloat16 [512, 29696], P('row', 'col')
- input_grad: bfloat16 [512, 14848], P('col', 'row')
- weight_grad: bfloat16 [14848, 29696], P('row', 'col')
All inputs are finite; a program needn't handle non-finite values.
Results may differ from a plain program's by a relative error of at most 0.001.
Values may be sent and summed in bfloat16 or wider, within the bound.
A program may use at most 64 MiB of HBM per device.

v0:
```python
import jax
import jax.numpy as jnp
from jax import lax
from jax.sharding import PartitionSpec as P


def body(inputs, weight, cotangent):
    gathered = lax.all_gather(inputs, "col", axis=0, tiled=True)
    contract_first = (((0,), (0,)), ((), ()))
    contract_last = (((1,), (1,)), ((), ()))
    token_block = gathered
    output = lax.psum_scatter(
        jnp.dot(token_block, weight, preferred_element_type=jnp.float32),
        "row",
        scatter_dimension=0,
        tiled=True,
    ).astype(jnp.bfloat16)
    collected = lax.all_gather(cotangent, "row", axis=0, tiled=True)
    weight_grad = lax.dot_general(
        gathered, collected, contract_first, preferred_element_type=jnp.float32
    )
    token_block = collected
    input_grad = lax.psum_scatter(
        lax.dot_general(token_block, weight, contract_last, preferred_element_type=jnp.float32),
        "col",
        scatter_dimension=0,
        tiled=True,
    )
    return (output, input_grad.astype(jnp.bfloat16), weight_grad.astype(jnp.bfloat16))


def solution(mesh):
    placed = (P("col", "row"), P("row", "col"), P("row", "col"))
    return jax.shard_map(
        body,
        mesh=mesh,
        in_specs=placed,
        out_specs=(P("row", "col"), P("col", "row"), P("row", "col")),
        check_vma=False,
    )
```

profile of v0, /device:TPU:40, one launch (start us, length us, event | category | flops | bytes accessed | tf_op | source)
XLA Modules:
  0.0 445.2 jit_solution(3341694522794693875)
XLA Ops:
  7.2 0.0 copy-start
  7.2 0.0 reduce-scatter.3.cloned.1.call-start
  7.2 51.0 %all_gather.6 = bf16[512,928]{1,0:T(8,128)(2,1)S(1)} all-gather(bf16[16,928]{1,0:T(8,128)(2,1)} %param.3), channel_id=1, replica_groups=mesh['row'=16,'col'=32] {'col'}, dimensions={0}, use_global_device_ids=true | all-gather | bytes 979968 | tf_op jit(solution)/shard_map/all_gather | solution.py:8
  58.3 0.0 copy-done
  58.3 2.6 fusion
  60.9 0.0 copy-start.2
  60.9 0.0 reduce-scatter.3.cloned.1.call-update
  60.9 0.0 reduce-scatter.5.cloned.1.call-start
  60.9 0.8 copy-done.2
  61.7 47.9 %all_gather.7 = bf16[512,928]{1,0:T(8,128)(2,1)S(1)} all-gather(bf16[32,928]{1,0:T(8,128)(2,1)S(1)} %copy-done.2), channel_id=1, replica_groups=mesh['row'=16,'col'=32] {'row'}, dimensions={0}, use_global_device_ids=true | all-gather | bytes 1009664 | tf_op jit(solution)/shard_map/all_gather | solution.py:18
  109.6 0.0 copy-start.1
  109.6 1.0 copy-done.1
  110.6 2.6 fusion.1
  113.2 0.0 reduce-scatter.5.cloned.1.call-update
  113.2 3.7 convolution_convert_fusion
  116.9 169.1 %reduce-scatter.3.cloned.1.call-done = f32[32,928]{1,0:T(8,128)} async-done(((f32[512,928]{1,0:T(8,128)}), f32[32,928]{1,0:T(8,128)}) %reduce-scatter.3.cloned.1.call-update) | async-done | bytes 118800 | tf_op jit(solution)/shard_map/reduce_scatter | solution.py:12
  286.0 1.5 convert_element_type.9
  287.6 149.4 %reduce-scatter.5.cloned.1.call-done = f32[16,928]{1,0:T(8,128)} async-done(((f32[512,928]{1,0:T(8,128)}), f32[16,928]{1,0:T(8,128)}) %reduce-scatter.5.cloned.1.call-update) | async-done | bytes 59408 | tf_op jit(solution)/shard_map/reduce_scatter | solution.py:23
  436.9 1.5 convert_element_type.10
Async XLA Ops:
  7.2 51.1 %copy-start = (bf16[928,928]{1,0:T(8,128)(2,1)S(1)}, bf16[928,928]{1,0:T(8,128)(2,1)}, u32[]{:S(2)}) copy-start(bf16[928,928]{1,0:T(8,128)(2,1)} %param.4) | copy-start | bytes 5167108
  7.2 278.9 %reduce-scatter.3.cloned.1.call-start = ((), (), s32[]{:S(2)}) async-start(), calls=%async_computation.2 | async-start | bytes 2228224 | tf_op jit(solution)/shard_map/reduce_scatter | solution.py:12
  60.9 0.8 copy-start.2
  60.9 376.1 %reduce-scatter.5.cloned.1.call-start = ((), (), s32[]{:S(2)}) async-start(), calls=%async_computation.3 | async-start | bytes 2162688 | tf_op jit(solution)/shard_map/reduce_scatter | solution.py:23
  109.6 1.0 copy-start.1
Sparse Core Ops, SparseCore 0:
  61.0 224.9 reduce-scatter.2
  289.1 147.8 reduce-scatter.4
where the time goes:
time: 446 us; the launch traced here: 445 us
  waiting for transfers between devices  319 us (72%)
  blocking collectives  99 us (22%)
  between operations  14.1 us (3%)
  matrix products  8.85 us (2%)
    reduce_scatter x1, waiting for transfers between devices, body(): lax.psum_scatter(jnp.dot(token_block, weight, preferred_element_type=jnp....  169 us
    reduce_scatter x1, waiting for transfers between devices, body(): lax.psum_scatter(lax.dot_general(token_block, weight, contract_last, pref...  149 us
    all_gather x1, blocking collectives, body(): gathered = lax.all_gather(inputs, 'col', axis=0, tiled=True)  51 us
    all_gather x1, blocking collectives, body(): collected = lax.all_gather(cotangent, 'row', axis=0, tiled=True)  47.9 us
  transfers between devices with their start and end apart: 2, of which 2 were waited for; matrix products, arithmetic and copies ran while one was open for 2% of the time, Pallas kernels for 0%

commit v1 on v0

v1 whole, which is shorter than its diff:
```python
import jax
import jax.numpy as jnp
from jax import lax
from jax.experimental import pallas as pl
from jax.experimental.pallas import tpu as pltpu
from jax.sharding import PartitionSpec as P

MESH = pl.DeviceIdType.MESH
BF, F32 = jnp.bfloat16, jnp.float32
W = 928
LANES = 1024
SPAN = 173.0
TILES = ((0, 256), (256, 512), (512, 768), (768, 928))


def encode(ref, v):
    a = jnp.abs(v)
    top = jnp.maximum(jnp.max(a, axis=1, keepdims=True) * 1.01, 1e-30).astype(BF).astype(F32)
    code = jnp.exp(a * (SPAN / top) - SPAN / 2)
    ref[:, :W] = jnp.where(v < 0, -code, code).astype(BF)
    ref[:, W:] = jnp.broadcast_to(top, (v.shape[0], LANES - W)).astype(BF)


def decode(coded):
    top = coded[:, W:W + 1].astype(F32)
    code = coded[:, :W].astype(F32)
    a = (jnp.log(jnp.abs(code)) + SPAN / 2) * (top / SPAN)
    return jnp.where(code < 0, -a, a)


def kernel(x_hbm, w_hbm, c_hbm, out_hbm, ig_hbm, wg_hbm,
           G, C, WV, P1, P2, WG, RB, SB, ZB, SR, X1, X2, ZL, OB, IB, ssem, rsem, lsem):
    row, col = lax.axis_index("row"), lax.axis_index("col")
    zh, y = row // 8, row % 8
    x, zl, core = col // 8, (col // 2) % 4, col % 2
    yp, ym = (y + 1) % 8, (y + 7) % 8
    xp, xm, xf = (x + 1) % 4, (x + 3) % 4, (x + 2) % 4
    zp = 1 - zh

    def at(zh_=zh, y_=y, x_=x, zl_=zl, core_=core):
        return (zh_ * 8 + y_, (x_ * 4 + zl_) * 2 + core_)

    right, left, far = at(y_=yp), at(y_=ym), at(zh_=zp)
    xright, xleft, sib = at(x_=xp), at(x_=xm), at(core_=1 - core)
    zpeer = [None] + [at(zl_=(zl + k) % 4) for k in (1, 2, 3)]
    ids, sent = {}, []

    def copy(name, src, dst, dev):
        n = ids.setdefault(name, len(ids))
        return pltpu.make_async_remote_copy(
            src_ref=src, dst_ref=dst, send_sem=ssem.at[n], recv_sem=rsem.at[n],
            device_id=dev, device_id_type=MESH)

    def send(name, src, dst, dev):
        c = copy(name, src, dst, dev)
        c.start()
        sent.append(c)

    def recv(name, dst):
        copy(name, dst, dst, sib).wait_recv()

    own_g = G.at[x * 4 + zl, core]
    own_c = C.at[zh, y]
    load_c = pltpu.make_async_copy(c_hbm, own_c, lsem.at[0])
    load_g = pltpu.make_async_copy(x_hbm, own_g, lsem.at[1])
    load_w = pltpu.make_async_copy(w_hbm, WV, lsem.at[2])
    load_c.start()
    load_g.start()
    barrier = pltpu.get_barrier_semaphore()
    peers = [right, left, far, xright, xleft, sib] + zpeer[1:]
    for dev in peers:
        pl.semaphore_signal(barrier, inc=1, device_id=dev, device_id_type=MESH)
    load_w.start()
    load_c.wait()
    load_g.wait()
    pl.semaphore_wait(barrier, len(peers))

    def gx(xx, lo, n, cc=core):
        return G.at[pl.ds(xx * 4 + lo, n), cc]

    def send_g(name, xx, lo, n, dev):
        send(name, gx(xx, lo, n), gx(xx, lo, n), dev)

    def cs(sub, yy):
        return C.at[zh if sub == 0 else zp, yy % 8]

    def ring_send(sub, sign, s):
        ref = cs(sub, y + 8 - sign * s)
        send(("k", sub, sign, s), ref, ref, right if sign > 0 else left)

    def ring_recv(sub, sign, s):
        recv(("k", sub, sign, s), cs(sub, y + 8 - sign * (s + 1)))

    ring_send(0, 1, 0)
    ring_send(0, -1, 0)
    for k in (1, 2, 3):
        send(("iz", k), own_g, own_g, zpeer[k])
    send("kz", own_c, own_c, far)

    for k in (1, 2, 3):
        recv(("iz", k), G.at[x * 4 + (zl + 4 - k) % 4, core])
    send_g("xp0", x, 0, 4, xright)
    send_g("xm0", x, 0, 4, xleft)
    send_g("s0", x, 0, 4, sib)
    for sign in (1, -1):
        ring_recv(0, sign, 0)
        ring_send(0, sign, 1)
    recv("kz", C.at[zp, y])
    for sign in (1, -1):
        ring_send(1, sign, 0)
    recv("xp0", gx(xm, 0, 4))
    send_g("xp1", xm, 0, 2, xright)
    send_g("s1", xm, 0, 4, sib)
    recv("xm0", gx(xp, 0, 4))
    send_g("xm1", xp, 2, 2, xleft)
    send_g("s2", xp, 0, 4, sib)
    for sign in (1, -1):
        ring_recv(0, sign, 1)
        ring_send(0, sign, 2)
    for sign in (1, -1):
        ring_recv(1, sign, 0)
        ring_send(1, sign, 1)
    recv("xp1", gx(xf, 0, 2))
    send_g("s3", xf, 0, 2, sib)
    recv("xm1", gx(xf, 2, 2))
    send_g("s4", xf, 2, 2, sib)
    load_w.wait()
    other = 1 - core
    recv("s0", gx(x, 0, 4, other))
    recv("s1", gx(xm, 0, 4, other))
    recv("s2", gx(xp, 0, 4, other))
    ring_recv(0, 1, 2)
    ring_send(0, 1, 3)
    recv("s3", gx(xf, 0, 2, other))
    recv("s4", gx(xf, 2, 2, other))

    g = G[...].reshape(512, W)
    for lo, hi in TILES:
        P1[:, lo:hi] = jnp.dot(g, WV[:, lo:hi], preferred_element_type=F32)

    def part(sub, yy):
        first = ((zh if sub == 0 else zp) * 8 + yy % 8) * 32
        return P1[pl.ds(pl.multiple_of(first, 32), 32), :]

    def first_step(sub, sign):
        return 0 if (sub == 1) == (sign > 0) else 1

    def red(sub, sign, s):
        d = 0 if sign > 0 else 1
        v = part(sub, y + 8 + sign * (4 - s))
        if s > first_step(sub, sign):
            recv(("r", sub, sign, s - 1), RB.at[d, sub, s - 1])
            v = v + decode(RB[d, sub, s - 1])
        encode(SB.at[d, sub, s], v)
        send(("r", sub, sign, s), SB.at[d, sub, s], RB.at[d, sub, s], right if sign > 0 else left)

    red(1, 1, 0)
    red(0, -1, 0)
    red(1, -1, 1)
    red(0, 1, 1)
    for sign in (1, -1):
        ring_recv(1, sign, 1)
        ring_send(1, sign, 2)
    red(1, 1, 1)
    ring_recv(0, -1, 2)
    ring_recv(0, 1, 3)
    ring_recv(1, -1, 2)
    ring_send(1, -1, 3)
    red(0, -1, 1)
    red(1, 1, 2)
    red(1, -1, 2)
    ring_recv(1, 1, 2)
    ring_recv(1, -1, 3)

    c = C[...].reshape(512, W)
    for lo, hi in TILES:
        P2[:, :, :, lo:hi] = lax.dot_general(
            c, WV[lo:hi, :], (((1,), (1,)), ((), ())), preferred_element_type=F32
        ).reshape(16, 2, 16, hi - lo)
    order = (xf, xp, xm, x)
    for j, xx in enumerate(order):
        send(("s", j), P2.at[pl.ds(xx * 4, 4), other], SR.at[j], sib)
    red(0, -1, 2)
    red(0, 1, 2)
    red(1, 1, 3)
    red(1, -1, 3)

    def q(j, lo, n):
        v = P2[pl.ds(order[j] * 4 + lo, n), core] + SR[j, lo:lo + n]
        return v.reshape(n * 16, W)

    def xsend(name, slot, v, dev):
        encode(X1.at[slot], v)
        send(name, X1.at[slot], X2.at[slot], dev)

    recv(("s", 0), SR.at[0])
    xsend("x0", 0, q(0, 0, 2), xright)
    xsend("x1", 1, q(0, 2, 2), xleft)
    recv(("s", 1), SR.at[1])
    xsend("x2", 2, q(1, 2, 2), xright)
    recv(("s", 2), SR.at[2])
    xsend("x3", 3, q(2, 0, 2), xleft)
    red(0, -1, 3)
    red(0, 1, 3)
    recv("x0", X2.at[0])
    xsend("x4", 4, q(1, 0, 2) + decode(X2[0]), xright)
    recv("x1", X2.at[1])
    xsend("x5", 5, q(2, 2, 2) + decode(X2[1]), xleft)

    recv(("r", 1, 1, 3), RB.at[0, 1, 3])
    recv(("r", 1, -1, 3), RB.at[1, 1, 3])
    encode(ZB.at[0], part(1, y) + decode(RB[0, 1, 3]) + decode(RB[1, 1, 3]))
    send("rz", ZB.at[0], ZB.at[1], far)

    gg = G[...].reshape(512, W)
    cc = C[...].reshape(512, W)
    for lo, hi in TILES:
        WG[lo:hi, :] = lax.dot_general(
            gg[:, lo:hi], cc, (((0,), (0,)), ((), ())), preferred_element_type=F32
        ).astype(BF)
    store_wg = pltpu.make_async_copy(WG, wg_hbm, lsem.at[3])
    store_wg.start()

    recv(("s", 3), SR.at[3])
    recv("x2", X2.at[2])
    recv("x3", X2.at[3])
    hi_half = q(3, 2, 2) + decode(X2[2])
    lo_half = q(3, 0, 2) + decode(X2[3])
    recv("x4", X2.at[4])
    recv("x5", X2.at[5])
    P2[pl.ds(x * 4, 2), core] = (lo_half + decode(X2[4])).reshape(2, 16, W)
    P2[pl.ds(x * 4 + 2, 2), core] = (hi_half + decode(X2[5])).reshape(2, 16, W)
    for k in (1, 2, 3):
        encode(ZL.at[0, k - 1], P2[x * 4 + (zl + k) % 4, core])
        send(("z", k), ZL.at[0, k - 1], ZL.at[1, k - 1], zpeer[k])

    recv(("r", 0, 1, 3), RB.at[0, 0, 3])
    recv(("r", 0, -1, 3), RB.at[1, 0, 3])
    o = part(0, y) + decode(RB[0, 0, 3]) + decode(RB[1, 0, 3])
    recv("rz", ZB.at[1])
    OB[...] = (o + decode(ZB[1])).astype(BF)
    store_o = pltpu.make_async_copy(OB, out_hbm, lsem.at[4])
    store_o.start()

    v = P2[x * 4 + zl, core]
    for k in (1, 2, 3):
        recv(("z", k), ZL.at[1, k - 1])
        v = v + decode(ZL[1, k - 1])
    IB[...] = v.astype(BF)
    store_i = pltpu.make_async_copy(IB, ig_hbm, lsem.at[5])
    store_i.start()
    for s in sent:
        s.wait_send()
    store_wg.wait()
    store_o.wait()
    store_i.wait()
    assert len(ids) <= ssem.shape[0]


def body(inputs, weight, cotangent):
    any_ = pl.BlockSpec(memory_space=pl.ANY)
    return tuple(pl.pallas_call(
        kernel,
        out_shape=(
            jax.ShapeDtypeStruct((32, W), BF),
            jax.ShapeDtypeStruct((16, W), BF),
            jax.ShapeDtypeStruct((W, W), BF),
        ),
        in_specs=[any_] * 3,
        out_specs=(any_,) * 3,
        scratch_shapes=[
            pltpu.VMEM((16, 2, 16, W), BF),
            pltpu.VMEM((2, 8, 32, W), BF),
            pltpu.VMEM((W, W), BF),
            pltpu.VMEM((512, W), F32),
            pltpu.VMEM((16, 2, 16, W), F32),
            pltpu.VMEM((W, W), BF),
            pltpu.VMEM((2, 2, 4, 32, LANES), BF),
            pltpu.VMEM((2, 2, 4, 32, LANES), BF),
            pltpu.VMEM((2, 32, LANES), BF),
            pltpu.VMEM((4, 4, 16, W), F32),
            pltpu.VMEM((6, 32, LANES), BF),
            pltpu.VMEM((6, 32, LANES), BF),
            pltpu.VMEM((2, 3, 16, LANES), BF),
            pltpu.VMEM((32, W), BF),
            pltpu.VMEM((16, W), BF),
            pltpu.SemaphoreType.DMA((64,)),
            pltpu.SemaphoreType.DMA((64,)),
            pltpu.SemaphoreType.DMA((6,)),
        ],
        compiler_params=pltpu.CompilerParams(
            collective_id=0, has_side_effects=True, vmem_limit_bytes=40 * 2**20),
        cost_estimate=pl.CostEstimate(flops=2650000000, bytes_accessed=4000000, transcendentals=0),
    )(inputs, weight, cotangent))


def solution(mesh):
    placed = (P("col", "row"), P("row", "col"), P("row", "col"))
    return jax.shard_map(
        body,
        mesh=mesh,
        in_specs=placed,
        out_specs=(P("row", "col"), P("col", "row"), P("row", "col")),
        check_vma=False,
    )
```

time: 446 us -> 64.6 us (0.14)
  the two profiles are of different devices: /device:TPU:40 before, /device:TPU:6 now
where the time goes in v1:
time: 64.6 us; the launch traced here: 64.3 us
  Pallas kernels  58 us (90%)
  local copies, waits for them, and re-layouts  5.61 us (9%)
  between operations  0.65 us (1%)
    pallas_call x1, Pallas kernels, body(): pl.pallas_call(kernel, out_shape=(jax.ShapeDtypeStruct((32, W), BF), jax....  58 us
    unnamed x9, local copies, waits for them, and re-layouts  5.61 us

profile of v1, /device:TPU:6, one launch (start us, length us, event | category | flops | bytes accessed | tf_op | source)
XLA Modules:
  0.0 64.3 jit_solution(9287592944747400797)
XLA Ops:
  0.6 0.0 copy-start
  0.6 1.5 %copy-done = bf16[928,928]{1,0:T(8,128)(2,1)S(1)} copy-done((bf16[928,928]{1,0:T(8,128)(2,1)S(1)}, bf16[928,928]{1,0:T(8,128)(2,1)}, u32[]{:S(2)}) %copy-start) | copy-done | bytes 1722392
  2.2 0.0 copy-start.1
  2.2 0.8 %copy-done.1 = bf16[32,928]{1,0:T(8,128)(2,1)S(1)} copy-done((bf16[32,928]{1,0:T(8,128)(2,1)S(1)}, bf16[32,928]{1,0:T(8,128)(2,1)}, u32[]{:S(2)}) %copy-start.1) | copy-done | bytes 59416
  3.0 0.0 copy-start.2
  3.0 0.8 %copy-done.2 = bf16[16,928]{1,0:T(8,128)(2,1)S(1)} copy-done((bf16[16,928]{1,0:T(8,128)(2,1)S(1)}, bf16[16,928]{1,0:T(8,128)(2,1)}, u32[]{:S(2)}) %copy-start.2) | copy-done | bytes 29720
  3.8 58.0 %shard_map.58 = (bf16[32,928]{1,0:T(8,128)(2,1)S(1)}, bf16[16,928]{1,0:T(8,128)(2,1)S(1)}, bf16[928,928]{1,0:T(8,128)(2,1)S(1)}) custom-call(bf16[16,928]{1,0:T(8,128)(2,1)S(1)} %copy-done.2, bf16[928,928]{1,0:T(8,128)(2,1)S(1)} %copy-done, bf16[32,928]{1,0:T(8,128)(2,1)S(1)} %copy-done.1), custom_call_target="tpu_custom_call" | custom-call | flops 2649999872 | bytes 4000000 | tf_op jit(solution)/shard_map/pallas_call | solution.py:262
  61.8 0.6 copy.9
  62.4 0.6 copy.10
  63.1 1.2 %copy.11 = bf16[928,928]{1,0:T(8,128)(2,1)} copy(bf16[928,928]{1,0:T(8,128)(2,1)S(1)} %get-tuple-element.8) | data formatting | bytes 3444736
Async XLA Ops:
  0.6 1.5 %copy-start = (bf16[928,928]{1,0:T(8,128)(2,1)S(1)}, bf16[928,928]{1,0:T(8,128)(2,1)}, u32[]{:S(2)}) copy-start(bf16[928,928]{1,0:T(8,128)(2,1)} %w_hbm.1) | copy-start | bytes 5167108
  2.2 0.8 %copy-start.1 = (bf16[32,928]{1,0:T(8,128)(2,1)S(1)}, bf16[32,928]{1,0:T(8,128)(2,1)}, u32[]{:S(2)}) copy-start(bf16[32,928]{1,0:T(8,128)(2,1)} %c_hbm.1) | copy-start | bytes 178180
  3.0 0.8 %copy-start.2 = (bf16[16,928]{1,0:T(8,128)(2,1)S(1)}, bf16[16,928]{1,0:T(8,128)(2,1)}, u32[]{:S(2)}) copy-start(bf16[16,928]{1,0:T(8,128)(2,1)} %x_hbm.1) | copy-start | bytes 89092

commit v2 on v0

v2 whole, which is shorter than its diff:
```python
import jax
import jax.numpy as jnp
from jax import lax
from jax.experimental import pallas as pl
from jax.experimental.pallas import tpu as pltpu
from jax.sharding import PartitionSpec as P

MESH = pl.DeviceIdType.MESH
BF, F32 = jnp.bfloat16, jnp.float32
W = 928
LANES = 1024
SPAN = 173.0
TILES = ((0, 256), (256, 512), (512, 768), (768, 928))
ORDER = ("K0", "I0", "KF", "IZ.2", "IZ.1", "IZ.3", "K.0", "GS", "SW", "KZ", "K.1", "GX.1", "GX.3", "GX.2", "KA.1", "KA.2", "K.2", "GR", "M1", "Q0", "F", "Q1", "KB.1", "KB.2", "K.3", "Q2", "R.1", "KR", "M2", "X.2", "X.1", "X.3", "X.0", "R.2", "Q3", "Y.2", "Y.1", "Y.3", "R.3", "W.0", "W.1", "Y.0", "IG", "W.2", "W.3", "OUT",)


def encode(ref, v):
    a = jnp.abs(v)
    top = jnp.maximum(jnp.max(a, axis=1, keepdims=True) * 1.01, 1e-30).astype(BF).astype(F32)
    code = jnp.exp(a * (SPAN / top) - SPAN / 2)
    ref[:, :W] = jnp.where(v < 0, -code, code).astype(BF)
    ref[:, W:] = jnp.broadcast_to(top, (v.shape[0], LANES - W)).astype(BF)


def decode(coded):
    top = coded[:, W:W + 1].astype(F32)
    code = coded[:, :W].astype(F32)
    a = (jnp.log(jnp.abs(code)) + SPAN / 2) * (top / SPAN)
    return jnp.where(code < 0, -a, a)


def kernel(x_hbm, w_hbm, c_hbm, out_ref, ig_ref, wg_ref,
           G, C, C2, WV, WS, P1, P2, RB, SB, ZB, X1, X2, ZL, ssem, rsem, lsem):
    row, col = lax.axis_index("row"), lax.axis_index("col")
    zh, y = row // 8, row % 8
    x, zl, core = col // 8, (col // 2) % 4, col % 2
    zp, other = 1 - zh, 1 - core
    xs = {1: (x + 1) % 4, 2: (x + 2) % 4, 3: (x + 3) % 4}

    def at(zh_=zh, y_=y, x_=x, zl_=zl, core_=core):
        return (zh_ * 8 + y_, (x_ * 4 + zl_) * 2 + core_)

    ydev = {n: at(y_=(y + 8 + n) % 8) for n in (1, -1, 2, -2)}
    xdev = {k: at(x_=xs[k]) for k in xs}
    zdev = {k: at(zl_=(zl + k) % 4) for k in (1, 2, 3)}
    far, sib = at(zh_=zp), at(core_=other)
    ids, sent = {}, []

    def copy(name, src, dst, dev):
        n = ids.setdefault(name, len(ids))
        return pltpu.make_async_remote_copy(
            src_ref=src, dst_ref=dst, send_sem=ssem.at[n], recv_sem=rsem.at[n],
            device_id=dev, device_id_type=MESH)

    def send(name, src, dst, dev):
        c = copy(name, src, dst, dev)
        c.start()
        sent.append(c)

    def recv(name, dst):
        copy(name, dst, dst, sib).wait_recv()

    def g_at(k, j):
        return G.at[x * 4 + (zl + 4 - k) % 4 if j == 0 else xs[j] * 4 + (zl + 4 - k) % 4, core]

    def g_forward(k):
        for j in (1, 3, 2):
            send(("gx", k, j), g_at(k, 0), g_at(k, 0), xdev[j])

    def z_arrival(k):
        recv(("iz", k), g_at(k, 0))
        g_forward(k)

    def g_row(j, cc):
        return G.at[pl.ds((x if j == 0 else xs[j]) * 4, 4), cc]

    def g_sibling(j):
        send(("gs", j), g_row(j, core), g_row(j, core), sib)

    def x_arrival(j):
        for k in range(4):
            recv(("gx", k, 4 - j), g_at(k, j))
        g_sibling(j)

    def g_complete():
        for j in range(4):
            recv(("gs", j), g_row(j, other))

    def c_at(sub, yy):
        return C.at[zh if sub == 0 else zp, yy % 8]

    def c_half(sub, yy, sign):
        return C.at[zh if sub == 0 else zp, yy % 8, 0 if sign > 0 else 1]

    def k_ref(sign, s):
        yy = y + 8 - sign * s
        return c_at(0, yy) if s < 4 else c_half(0, yy, sign)

    def k_send(sign, s):
        ref = k_ref(sign, s) if s < 3 else c_half(0, y + 8 - sign * s, sign)
        send(("k", sign, s), ref, ref, ydev[sign])

    def k_start():
        for sign in (1, -1):
            k_send(sign, 0)

    def k_step(s):
        for sign in (1, -1):
            recv(("k", sign, s), k_ref(sign, s + 1))
            if s < 3:
                k_send(sign, s + 1)
        if s == 3:
            send("ks", C.at[zh, :, other], C2.at[zh], sib)

    def k_sibling(yy):
        send(("ks", yy), c_at(1, y + 8 + yy).at[other], C2.at[zp, (y + 8 + yy) % 8], sib)

    def k_far():
        recv("kz", c_at(1, y))
        for n in (2, 1):
            for sign in (1, -1):
                send(("ka", n, sign), c_at(1, y), c_at(1, y), ydev[n * sign])
        k_sibling(0)

    def k_near(n):
        for sign in (1, -1):
            recv(("ka", n, sign), c_at(1, y + 8 - n * sign))
        if n == 2:
            for sign in (1, -1):
                ref = c_half(1, y + 8 - 2 * sign, sign)
                send(("kb", 2, sign), ref, ref, ydev[2 * sign])
            for sign in (1, -1):
                ref = c_at(1, y + 8 - 2 * sign)
                send(("kb", 1, sign), ref, ref, ydev[sign])
        for sign in (1, -1):
            k_sibling(-n * sign)

    def k_distant(n):
        for sign in (1, -1):
            if n == 1:
                recv(("kb", 1, sign), c_at(1, y + 8 - 3 * sign))
                k_sibling(-3 * sign)
            else:
                recv(("kb", 2, sign), c_half(1, y + 4, sign))
        if n == 2:
            k_sibling(4)

    def w_sibling():
        send("w", w_hbm, WS, sib)

    def m_output():
        load_w.wait()
        g = G[...].reshape(512, W)
        for lo, hi in TILES:
            P1[:, lo:hi] = jnp.dot(g, WV[:, lo:hi], preferred_element_type=F32)

    def part(sub, yy, p=None):
        first = ((zh if sub == 0 else zp) * 8 + yy % 8) * 32 + (16 if p == 1 else 0)
        n = 32 if p is None else 16
        return P1[pl.ds(pl.multiple_of(first, 16), n), :]

    def r_send(*parts):
        for name, n, sign, v, dev in parts:
            encode(SB.at[n, 0 if sign > 0 else 1, pl.ds(0, v.shape[0])], v)
        for name, n, sign, v, dev in parts:
            at_ = (n, 0 if sign > 0 else 1, pl.ds(0, v.shape[0]))
            send((name, sign), SB.at[at_], RB.at[at_], dev)

    def r_recv(name, n, sign, rows=32):
        recv((name, sign), RB.at[n, 0 if sign > 0 else 1, pl.ds(0, rows)])

    def r_value(n, sign, rows=32):
        return decode(RB[n, 0 if sign > 0 else 1, :rows])

    def with_half(v, half, sign):
        zero = jnp.zeros_like(half)
        return v + jnp.concatenate([half, zero] if sign > 0 else [zero, half], axis=0)

    def r_start():
        r_send(*[("r0", 0, sign, part(0, y + 4, 0 if sign > 0 else 1), ydev[sign]) for sign in (1, -1)])

    def r_step(s):
        rows = 16 if s == 1 else 32
        for sign in (1, -1):
            r_recv(f"r{s - 1}", s - 1, sign, rows)
        sums = []
        for sign in (1, -1):
            v, got = part(0, y + 8 + sign * (4 - s)), r_value(s - 1, sign, rows)
            v = with_half(v, got, sign) if s == 1 else v + got
            sums.append((f"r{s}", s, sign, v, ydev[sign]))
        r_send(*sums)

    def q_start():
        r_send(
            *[("q4", 5, sign, part(1, y + 4, 0 if sign > 0 else 1), ydev[2 * sign]) for sign in (1, -1)],
            *[("q3", 4, sign, part(1, y + 8 + 3 * sign), ydev[sign]) for sign in (1, -1)])

    def q_near():
        r_send(*[("q1", 6, sign, part(1, y + 8 + sign), ydev[sign]) for sign in (1, -1)])

    def q_relay():
        for sign in (1, -1):
            r_recv("q3", 4, sign)
            r_recv("q4", 5, sign, 16)
        sums = []
        for sign in (1, -1):
            v = part(1, y + 8 + 2 * sign) + r_value(4, sign)
            sums.append(("q2", 7, sign, with_half(v, r_value(5, sign, 16), sign), ydev[2 * sign]))
        r_send(*sums)

    def q_far():
        for sign in (1, -1):
            r_recv("q1", 6, sign)
            r_recv("q2", 7, sign)
        v = part(1, y)
        for sign in (1, -1):
            v = v + r_value(6, sign) + r_value(7, sign)
        encode(ZB.at[0], v)
        send("rz", ZB.at[0], ZB.at[1], far)

    def finish_output():
        for sign in (1, -1):
            r_recv("r3", 3, sign)
        v = part(0, y) + r_value(3, 1) + r_value(3, -1)
        recv("rz", ZB.at[1])
        out_ref[...] = (v + decode(ZB[1])).astype(BF)

    def k_complete():
        recv("ks", C2.at[zh])
        for yy in range(-3, 5):
            recv(("ks", yy), C2.at[zp, (y + 8 + yy) % 8])

    def m_input_grad():
        recv("w", WS)
        c = C[:, :, core].reshape(256, W)
        c2 = C2[...].reshape(256, W)
        dims = (((1,), (1,)), ((), ()))
        for lo, hi in TILES:
            t = lax.dot_general(c, WV[lo:hi, :], dims, preferred_element_type=F32)
            t += lax.dot_general(c2, WS[lo:hi, :], dims, preferred_element_type=F32)
            P2[:, :, lo:hi] = t.reshape(16, 16, hi - lo)

    def x_send(dz):
        zd = (zl + dz) % 4
        for j in (1, 3, 2):
            encode(X1.at[dz, j - 1], P2[xs[j] * 4 + zd])
        for j in (1, 3, 2):
            send(("x", dz, j), X1.at[dz, j - 1], X2.at[dz, j - 1], xdev[j])

    def x_sum(dz):
        for j in (1, 3, 2):
            recv(("x", dz, j), X2.at[dz, j - 1])
        v = P2[x * 4 + (zl + dz) % 4]
        for j in (1, 3, 2):
            v = v + decode(X2[dz, j - 1])
        if dz == 0:
            P2[x * 4 + zl] = v
        else:
            encode(ZL.at[0, dz - 1], v)
            send(("z", dz), ZL.at[0, dz - 1], ZL.at[1, dz - 1], zdev[dz])

    def finish_input_grad():
        v = P2[x * 4 + zl]
        for k in (1, 2, 3):
            recv(("z", k), ZL.at[1, k - 1])
            v = v + decode(ZL[1, k - 1])
        ig_ref[...] = v.astype(BF)

    def m_weight_grad(n):
        lo, hi = TILES[n]
        g = G[:, :, :, lo:hi].reshape(512, hi - lo)
        c = C[...].reshape(512, W)
        wg_ref[lo:hi, :] = lax.dot_general(
            g, c, (((0,), (0,)), ((), ())), preferred_element_type=F32).astype(BF)

    own_g = g_at(0, 0)
    loads = [pltpu.make_async_copy(c_hbm.at[pl.ds(16 * p, 16)], C.at[zh, y, p], lsem.at[p]) for p in (0, 1)]
    loads.append(pltpu.make_async_copy(x_hbm, own_g, lsem.at[6]))
    load_w = pltpu.make_async_copy(w_hbm, WV, lsem.at[2])
    for load in loads:
        load.start()
    barrier = pltpu.get_barrier_semaphore()
    peers = list(ydev.values()) + list(xdev.values()) + list(zdev.values()) + [far, sib]
    for dev in peers:
        pl.semaphore_signal(barrier, inc=1, device_id=dev, device_id_type=MESH)
    load_w.start()
    for load in loads:
        load.wait()
    pl.semaphore_wait(barrier, len(peers))

    def start_inputs():
        for k in (2, 1, 3):
            send(("iz", k), own_g, own_g, zdev[k])
        g_forward(0)

    def start_cotangent():
        k_start()

    def start_far():
        send("kz", c_at(0, y), c_at(0, y), far)

    run = {
        "I0": start_inputs, "K0": start_cotangent, "KF": start_far,
        "IZ": z_arrival, "GS": lambda: g_sibling(0), "GX": x_arrival, "GR": g_complete,
        "K": k_step, "KZ": k_far, "KA": k_near, "KB": k_distant, "KR": k_complete, "SW": w_sibling,
        "M1": m_output, "F": r_start, "R": r_step, "Q0": q_start, "Q1": q_near, "Q2": q_relay, "Q3": q_far,
        "OUT": finish_output, "M2": m_input_grad, "X": x_send, "Y": x_sum, "IG": finish_input_grad,
        "W": m_weight_grad,
    }
    for token in ORDER:
        name, *numbers = token.split(".")
        run[name](*map(int, numbers))
    if "M1" not in ORDER:
        load_w.wait()
    for s in sent:
        s.wait_send()
    assert len(ids) <= ssem.shape[0]


def body(inputs, weight, cotangent):
    any_ = pl.BlockSpec(memory_space=pl.ANY)
    hbm = pl.BlockSpec(memory_space=pltpu.HBM)
    results = pl.pallas_call(
        kernel,
        out_shape=tuple(pltpu.VMEM(shape, BF) for shape in ((32, W), (16, W), (W, W))),
        in_specs=[hbm] * 3,
        out_specs=(pl.BlockSpec(memory_space=pltpu.VMEM),) * 3,
        scratch_shapes=[
            pltpu.VMEM((16, 2, 16, W), BF),
            pltpu.VMEM((2, 8, 2, 16, W), BF),
            pltpu.VMEM((2, 8, 16, W), BF),
            pltpu.VMEM((W, W), BF),
            pltpu.VMEM((W, W), BF),
            pltpu.VMEM((512, W), F32),
            pltpu.VMEM((16, 16, W), F32),
            pltpu.VMEM((8, 2, 32, LANES), BF),
            pltpu.VMEM((8, 2, 32, LANES), BF),
            pltpu.VMEM((2, 32, LANES), BF),
            pltpu.VMEM((4, 3, 16, LANES), BF),
            pltpu.VMEM((4, 3, 16, LANES), BF),
            pltpu.VMEM((2, 3, 16, LANES), BF),
            pltpu.SemaphoreType.DMA((112,)),
            pltpu.SemaphoreType.DMA((112,)),
            pltpu.SemaphoreType.DMA((8,)),
        ],
        compiler_params=pltpu.CompilerParams(
            collective_id=0, has_side_effects=True, vmem_limit_bytes=60 * 2**20),
        cost_estimate=pl.CostEstimate(flops=2650000000, bytes_accessed=4000000, transcendentals=0),
    )(inputs, weight, cotangent)
    return tuple(results)


def solution(mesh):
    placed = (P("col", "row"), P("row", "col"), P("row", "col"))
    return jax.shard_map(
        body,
        mesh=mesh,
        in_specs=placed,
        out_specs=(P("row", "col"), P("col", "row"), P("row", "col")),
        check_vma=False,
    )
```

time: 446 us -> 55.6 us (0.12)
  the two profiles are of different devices: /device:TPU:40 before, /device:TPU:6 now
where the time goes in v2:
time: 55.6 us; the launch traced here: 55.5 us
  Pallas kernels  52.3 us (94%)
  local copies, waits for them, and re-layouts  2.5 us (4%)
  between operations  0.64 us (1%)
    pallas_call x1, Pallas kernels, body(): pl.pallas_call(kernel, out_shape=tuple((pltpu.VMEM(shape, BF) for shape i...  52.3 us
    unnamed x3, local copies, waits for them, and re-layouts  2.5 us

profile of v2, /device:TPU:6, one launch (start us, length us, event | category | flops | bytes accessed | tf_op | source)
XLA Modules:
  0.0 55.5 jit_solution(17191817040032124808)
XLA Ops:
  0.6 52.3 %shard_map.58 = (bf16[32,928]{1,0:T(8,128)(2,1)S(1)}, bf16[16,928]{1,0:T(8,128)(2,1)S(1)}, bf16[928,928]{1,0:T(8,128)(2,1)S(1)}) custom-call(bf16[16,928]{1,0:T(8,128)(2,1)} %x_hbm.1, bf16[928,928]{1,0:T(8,128)(2,1)} %w_hbm.1, bf16[32,928]{1,0:T(8,128)(2,1)} %c_hbm.1), custom_call_target="tpu_custom_call" | custom-call | flops 2649999872 | bytes 4000000 | tf_op jit(solution)/shard_map/pallas_call | solution.py:323
  53.0 0.6 %copy.9 = bf16[32,928]{1,0:T(8,128)(2,1)} copy(bf16[32,928]{1,0:T(8,128)(2,1)S(1)} %get-tuple-element.3) | data formatting | bytes 118784
  53.6 0.6 %copy.10 = bf16[16,928]{1,0:T(8,128)(2,1)} copy(bf16[16,928]{1,0:T(8,128)(2,1)S(1)} %get-tuple-element.4) | data formatting | bytes 59392
  54.2 1.2 %copy.11 = bf16[928,928]{1,0:T(8,128)(2,1)} copy(bf16[928,928]{1,0:T(8,128)(2,1)S(1)} %get-tuple-element.5) | data formatting | bytes 3444736

commit v3 on v2

--- a/solution.py
+++ b/solution.py
@@ -11,7 +11,9 @@
 LANES = 1024
 SPAN = 173.0
 TILES = ((0, 256), (256, 512), (512, 768), (768, 928))
-ORDER = ("K0", "I0", "KF", "IZ.2", "IZ.1", "IZ.3", "K.0", "GS", "SW", "KZ", "K.1", "GX.1", "GX.3", "GX.2", "KA.1", "KA.2", "K.2", "GR", "M1", "Q0", "F", "Q1", "KB.1", "KB.2", "K.3", "Q2", "R.1", "KR", "M2", "X.2", "X.1", "X.3", "X.0", "R.2", "Q3", "Y.2", "Y.1", "Y.3", "R.3", "W.0", "W.1", "Y.0", "IG", "W.2", "W.3", "OUT",)
+ORDER = (
+    "K0", "I0", "KF", "IZ.2", "IZ.1", "IZ.3", "K.0", "GS", "SW", "KZ", "K.1", "GX.1", "GX.3", "GX.2", "KA.1", "KA.2", "K.2", "GR", "M1", "Q0", "F", "Q1", "KB.1", "KB.2", "K.3", "Q2", "R.1", "KR", "M2", "X.2", "X.1", "X.3", "X.0", "R.2", "Q3", "Y.2", "Y.1", "Y.3", "R.3", "W.0", "W.1", "Y.0", "W.2", "W.3", "IG", "OUT",
+)
 
 
 def encode(ref, v):
@@ -192,7 +194,8 @@
 
     def q_start():
         r_send(
-            *[("q4", 5, sign, part(1, y + 4, 0 if sign > 0 else 1), ydev[2 * sign]) for sign in (1, -1)],
+            *[("q4", 5, sign, part(1, y + 4, 0 if sign > 0 else 1), ydev[2 * sign]) for sign in (1, -1)])
+        r_send(
             *[("q3", 4, sign, part(1, y + 8 + 3 * sign), ydev[sign]) for sign in (1, -1)])
 
     def q_near():

time: 55.6 us -> 55.8 us (level)
  no operation moved by 1% of the time
where the time goes in v3:
time: 55.8 us; the launch traced here: 55.4 us
  Pallas kernels  52.3 us (94%)
  local copies, waits for them, and re-layouts  2.5 us (4%)
  between operations  0.64 us (1%)
    pallas_call x1, Pallas kernels, body(): pl.pallas_call(kernel, out_shape=tuple((pltpu.VMEM(shape, BF) for shape i...  52.3 us
    unnamed x3, local copies, waits for them, and re-layouts  2.5 us

profile of v3, /device:TPU:6, one launch (start us, length us, event | category | flops | bytes accessed | tf_op | source)
XLA Modules:
  0.0 55.4 jit_solution(3613873620366767257)
XLA Ops:
  0.6 52.3 %shard_map.58 = (bf16[32,928]{1,0:T(8,128)(2,1)S(1)}, bf16[16,928]{1,0:T(8,128)(2,1)S(1)}, bf16[928,928]{1,0:T(8,128)(2,1)S(1)}) custom-call(bf16[16,928]{1,0:T(8,128)(2,1)} %x_hbm.1, bf16[928,928]{1,0:T(8,128)(2,1)} %w_hbm.1, bf16[32,928]{1,0:T(8,128)(2,1)} %c_hbm.1), custom_call_target="tpu_custom_call" | custom-call | flops 2649999872 | bytes 4000000 | tf_op jit(solution)/shard_map/pallas_call | solution.py:326
  52.9 0.6 %copy.9 = bf16[32,928]{1,0:T(8,128)(2,1)} copy(bf16[32,928]{1,0:T(8,128)(2,1)S(1)} %get-tuple-element.3) | data formatting | bytes 118784
  53.5 0.6 %copy.10 = bf16[16,928]{1,0:T(8,128)(2,1)} copy(bf16[16,928]{1,0:T(8,128)(2,1)S(1)} %get-tuple-element.4) | data formatting | bytes 59392
  54.1 1.2 %copy.11 = bf16[928,928]{1,0:T(8,128)(2,1)} copy(bf16[928,928]{1,0:T(8,128)(2,1)S(1)} %get-tuple-element.5) | data formatting | bytes 3444736
